TPU v7x, 128 devices: a whole 4x4x4 slice. The times are simulated.
128 devices in a mesh: var: 4 (over z), samp: 32 (over x, y, core).
Axes of the slice: x: 4, y: 4, z: 4, core: 2. Of those that a mesh axis runs over, the one named last changes fastest.
Arguments:
- genotypes: int32 [3072, 98304], P('var', 'samp'), may hold values from 0 to 2, as said below
- called: int32 [3072, 98304], P('var', 'samp'), may hold values from 0 to 1
- dosage: int32 [98304, 1024], P(('samp', 'var')), may hold values from 0 to 200
- sample_order: int32 [128, 768], P(('samp', 'var')), may hold values from 0 to 767, each once within a row
- noise_ratio: float32 [16], replicated, may hold values from 0.5 to 4
- solution: float32 [98304, 16], P(('samp', 'var')), may hold values from -13 to 13
- residual: float32 [98304, 16], P(('samp', 'var')), may hold values from -13 to 13
- direction: float32 [98304, 16], P(('samp', 'var')), may hold values from -13 to 13
Outputs:
- solution_new: float32 [98304, 16], P(('samp', 'var'))
- residual_new: float32 [98304, 16], P(('samp', 'var'))
- direction_new: float32 [98304, 16], P(('samp', 'var'))
- scores: float32 [1024, 16], P(('var', 'samp'))
Inputs may be any that keep to these rules, and one draw needn't show every extreme that they name: `genotypes`: where called is 1, the count of one allele. `sample_order`: each row lists 0 to 767 once.
All inputs are finite; a program needn't handle non-finite values.
Results may differ from a plain program's by a relative error of at most 0.023.
Values may be sent and summed in bfloat16 or wider, within the bound.
A program may use at most 128 MiB of HBM per device.

v0:
```python
import math
import jax
import jax.numpy as jnp
from jax import lax
from jax.sharding import PartitionSpec as P

VARIANTS = 3072


def standard_form(raw_proj, called_proj, allele_sum, called_count):
    frequency = (allele_sum + 1.0) / (2.0 * called_count + 2.0)
    spread = jnp.sqrt(2.0 * frequency * (1.0 - frequency))
    loading = (raw_proj - 2.0 * frequency[:, None] * called_proj) / spread[:, None]
    return (frequency, spread, loading)


def body(genotypes, called, dosage, sample_order, noise_ratio, solution, residual, direction):
    coded = genotypes * called
    coded_b = coded.astype(jnp.bfloat16)
    called_b = called.astype(jnp.bfloat16)
    allele_sum = jnp.sum(coded, axis=1).astype(jnp.float32)
    called_count = jnp.sum(called, axis=1).astype(jnp.float32)
    quarter = direction.shape[0]
    samples = quarter * lax.axis_size("samp") * lax.axis_size("var")
    dosage_b = dosage.astype(jnp.bfloat16)
    dosage_sum = jnp.sum(dosage, axis=0).astype(jnp.float32)
    order_row = sample_order[0]
    direction_b = direction.astype(jnp.bfloat16)
    piece = lax.all_gather(direction_b, "var", axis=0, tiled=True)
    coded_cols = coded_b
    called_cols = called_b
    raw_proj = jnp.dot(coded_cols, piece, preferred_element_type=jnp.float32)
    called_proj = jnp.dot(called_cols, piece, preferred_element_type=jnp.float32)
    raw_proj, called_proj, allele_sum, called_count = (
        lax.psum(raw_proj.astype(jnp.bfloat16), "samp").astype(jnp.float32),
        lax.psum(called_proj.astype(jnp.bfloat16), "samp").astype(jnp.float32),
        lax.psum(allele_sum.astype(jnp.bfloat16), "samp").astype(jnp.float32),
        lax.psum(called_count.astype(jnp.bfloat16), "samp").astype(jnp.float32),
    )
    frequency, spread, loading = standard_form(raw_proj, called_proj, allele_sum, called_count)
    scaled_a = (loading / spread[:, None]).astype(jnp.bfloat16)
    scaled_b = (2.0 * frequency[:, None] * loading / spread[:, None]).astype(jnp.bfloat16)
    coded_cols = coded_b
    called_cols = called_b
    term = jnp.einsum("vs,vc->sc", coded_cols, scaled_a, preferred_element_type=jnp.float32)
    term = term - jnp.einsum("vs,vc->sc", called_cols, scaled_b, preferred_element_type=jnp.float32)
    back = lax.psum_scatter(
        (term / VARIANTS).astype(jnp.bfloat16), "var", scatter_dimension=0, tiled=True
    ).astype(jnp.float32)
    applied = noise_ratio[None, :] * direction + back
    res_norm, curvature = lax.psum(
        (jnp.sum(residual * residual, axis=0), jnp.sum(direction * applied, axis=0)),
        ("var", "samp"),
    )
    step_size = res_norm / (curvature + 1e-06)
    solution_new = solution + step_size[None, :] * direction
    residual_new = residual - step_size[None, :] * applied
    res_square = jnp.sum(residual_new * residual_new, axis=0)
    res_new_norm, sol_sum, sol_square = lax.psum(
        (res_square, jnp.sum(solution_new, axis=0), jnp.sum(solution_new * solution_new, axis=0)),
        ("var", "samp"),
    )
    picked = jnp.take(solution_new, order_row, axis=0).astype(jnp.bfloat16)
    cross_local = jnp.einsum("ij,ic->jc", dosage_b, picked, preferred_element_type=jnp.float32)
    cross_sum, dosage_sum = (
        lax.psum_scatter(cross_local, ("var", "samp"), scatter_dimension=0, tiled=True),
        lax.psum_scatter(dosage_sum, ("var", "samp"), scatter_dimension=0, tiled=True),
    )
    direction_new = residual_new + (res_new_norm / (res_norm + 1e-06))[None, :] * direction
    dose_freq = (dosage_sum / 100.0 + 1.0) / (2.0 * samples + 2.0)
    dose_spread = jnp.sqrt(2.0 * dose_freq * (1.0 - dose_freq))
    scale_norm = math.sqrt(samples) * jnp.sqrt(sol_square / samples + 1e-06)
    scores = (cross_sum / 100.0 - 2.0 * dose_freq[:, None] * sol_sum[None, :]) / (
        dose_spread[:, None] * scale_norm[None, :]
    )
    return (solution_new, residual_new, direction_new, scores)


def solution(mesh):
    placed = (
        P("var", "samp"),
        P("var", "samp"),
        P(("samp", "var"), None),
        P(("samp", "var"), None),
        P(),
        P(("samp", "var"), None),
        P(("samp", "var"), None),
        P(("samp", "var"), None),
    )
    return jax.shard_map(
        body,
        mesh=mesh,
        in_specs=placed,
        out_specs=(
            P(("samp", "var"), None),
            P(("samp", "var"), None),
            P(("samp", "var"), None),
            P(("var", "samp"), None),
        ),
        check_vma=False,
    )
```

profile of v0, /device:TPU:1, one launch (start us, length us, event | category | flops | bytes accessed | tf_op | source)
XLA Modules:
  0.0 401.3 jit_solution(4430301488992100264)
XLA Ops:
  7.2 0.8 convert_element_type.61
  8.0 11.4 %all_gather.3 = bf16[3072,16]{0,1:T(8,128)(2,1)S(1)} all-gather(bf16[768,16]{0,1:T(8,128)(2,1)S(1)} %convert_element_type.61), channel_id=1, replica_groups=mesh['var'=4,'samp'=32] {'var'}, dimensions={0}, use_global_device_ids=true | all-gather | bytes 122880 | tf_op jit(solution)/shard_map/all_gather | solution.py:29
  19.5 10.1 %multiply_reduce_fusion = (s32[768]{0:T(1024)S(1)}, s32[768]{0:T(1024)S(1)}, bf16[768,3072]{1,0:T(8,128)(2,1)}) fusion(s32[768,3072]{1,0:T(8,128)} %param.8, s32[768,3072]{1,0:T(8,128)} %param.9), kind=kLoop, calls=%fused_computation.1 | loop fusion | flops 9435648 | bytes 23599104 | tf_op jit(solution)/shard_map/reduce_sum | solution.py:21
  29.6 5.1 %fusion.10 = bf16[768,16]{0,1:T(8,128)(2,1)S(1)} fusion(bf16[3072,16]{0,1:T(8,128)(2,1)S(1)} %all_gather.3, s32[768,3072]{1,0:T(8,128)} %param.9), kind=kOutput, calls=%fused_computation.13 | convolution fusion | flops 77869056 | bytes 9560064 | tf_op jit(solution)/shard_map/dot_general | solution.py:33
  34.7 1.3 convolution_convert_fusion
  36.1 123.5 %all-reduce.4 = (bf16[768,16]{0,1:T(8,128)(2,1)S(1)}, bf16[768,16]{0,1:T(8,128)(2,1)S(1)}, bf16[768]{0:T(1024)(128)(2,1)S(1)}, bf16[768]{0:T(1024)(128)(2,1)S(1)}) all-reduce(bf16[768,16]{0,1:T(8,128)(2,1)S(1)} %fusion.10, bf16[768,16]{0,1:T(8,128)(2,1)S(1)} %convolution_convert_fusion, ...), channel_id=1, replica_groups=mesh['var'=4,'samp'=32] {'samp'}, use_global_device_ids=true, to_apply=%region_7.0 | all-reduce | flops 26112 | bytes 104448 | tf_op jit(solution)/shard_map/psum | solution.py:36
  159.6 4.6 %convolution_bitcast_fusion = f32[3072,16]{0,1:T(8,128)S(1)} fusion(s32[768,3072]{1,0:T(8,128)} %param.9, bf16[768,16]{0,1:T(8,128)(2,1)S(1)} %get-tuple-element.26, bf16[768,16]{0,1:T(8,128)(2,1)S(1)} %get-tuple-element.27, f32[768]{0:T(1024)S(1)} %get-tuple-element.40, f32[768]{0:T(1024)S(1)} %get-tuple-element.41), kind=kOutput, calls=%fused_computation.5 | convolution fusion | flops 77955072 | bytes 9689088 | tf_op jit(solution)/shard_map/vs,vc->sc/dot_general | solution.py:46
  164.2 0.3 slice-done.1
  164.5 1.4 fusion.1
  166.1 2.3 reduce_sum.77
  168.4 16.6 %reduce-scatter.3.cloned.1.call-done = bf16[768,16]{0,1:T(8,128)(2,1)} async-done(((bf16[3072,16]{0,1:T(8,128)(2,1)}), bf16[768,16]{0,1:T(8,128)(2,1)}) %reduce-scatter.3.cloned.1.call-update) | async-done | bytes 24592 | tf_op jit(solution)/shard_map/reduce_scatter | solution.py:47
  185.0 0.9 multiply_reduce_fusion.3
  186.0 66.8 %all-reduce.3 = (f32[16]{0:T(128)S(1)}, f32[16]{0:T(128)S(1)}) all-reduce(f32[16]{0:T(128)S(1)} %multiply_reduce_fusion.4, f32[16]{0:T(128)S(1)} %multiply_reduce_fusion.3), channel_id=1, replica_groups=mesh['var'=4,'samp'=32] {'var','samp'}, use_global_device_ids=true, to_apply=%region_1.0 | all-reduce | flops 32 | bytes 256 | tf_op jit(solution)/shard_map/psum | solution.py:51
  252.8 2.1 multiply_reduce_fusion.2
  254.9 0.6 copy-done.4
  255.5 0.2 copy.16
  255.7 1.9 gather_fusion
  257.6 1.1 fusion.7
  258.7 63.2 %all-reduce.2 = (f32[16]{0:T(128)S(1)}, f32[16]{0:T(128)S(1)}, f32[1024]{0:T(1024)S(1)}, f32[16]{0:T(128)S(1)}) all-reduce(f32[16]{0:T(128)S(1)} %get-tuple-element.31, f32[16]{0:T(128)} %get-tuple-element.34, f32[1024]{0:T(1024)S(1)} %convert_element_type.79, f32[16]{0:T(128)} %get-tuple-element.35), channel_id=1, replica_groups=mesh['var'=4,'samp'=32] {'var','samp'}, use_global_device_ids=true, to_apply=%region_12.0 | all-reduce | flops 1072 | bytes 8576 | tf_op jit(solution)/shard_map/psum | solution.py:59
  321.9 0.6 add_divide_fusion.1
  322.6 1.5 multiply_add_fusion
  324.2 68.9 %all-reduce.7.cloned.1.call-done = f32[1024,16]{0,1:T(8,128)} async-done(((f32[1024,16]{0,1:T(8,128)}), f32[1024,16]{0,1:T(8,128)}) %all-reduce.7.cloned.1.call-update) | async-done | bytes 65552
  393.0 0.8 fusion.20
  393.8 0.7 copy.17
  (36 shorter events, 0.4 us)
Async XLA Ops:
  7.2 177.9 %reduce-scatter.3.cloned.1.call-start = ((), (), s32[]{:S(2)}) async-start(), calls=%async_computation.1 | async-start | bytes 122880 | tf_op jit(solution)/shard_map/reduce_scatter | solution.py:47
  29.6 5.2 %copy-start = (bf16[768,3072]{1,0:T(8,128)(2,1)S(1)}, bf16[768,3072]{1,0:T(8,128)(2,1)}, u32[]{:S(2)}) copy-start(bf16[768,3072]{1,0:T(8,128)(2,1)} %get-tuple-element.33) | copy-start | bytes 14155780
  34.7 129.5 %slice-start = ((s8[4718592]{0:T(1024)(128)(4,1)}), s8[524288]{0:T(1024)(128)(4,1)S(1)}, s32[]{:S(2)}) async-start(s8[4718592]{0:T(1024)(128)(4,1)} %bitcast.12), calls=%async_computation.3 | async-start | bytes 1048576
  159.6 4.9 %slice-start.1 = ((s8[4718592]{0:T(1024)(128)(4,1)}), s8[4194304]{0:T(1024)(128)(4,1)S(1)}, s32[]{:S(2)}) async-start(s8[4718592]{0:T(1024)(128)(4,1)} %bitcast.12), calls=%async_computation.4 | async-start | bytes 8388608
  164.2 1.8 copy-start.3
  164.2 1.9 copy-start.6
  164.2 20.9 %copy-start.2 = (f32[768,16]{0,1:T(8,128)S(1)}, f32[768,16]{0,1:T(8,128)}, u32[]{:S(2)}) copy-start(f32[768,16]{0,1:T(8,128)} %param.15) | copy-start | bytes 147460
  164.2 20.9 %copy-start.7 = (f32[16]{0:T(128)S(1)}, f32[16]{0:T(128)}, u32[]{:S(2)}) copy-start(f32[16]{0:T(128)} %param.12) | copy-start | bytes 196
  164.2 88.6 %copy-start.5 = (f32[768,16]{0,1:T(8,128)S(1)}, f32[768,16]{0,1:T(8,128)}, u32[]{:S(2)}) copy-start(f32[768,16]{0,1:T(8,128)} %param.13) | copy-start | bytes 147460
  165.8 91.7 %copy-start.1 = (s32[768,1024]{1,0:T(8,128)S(1)}, s32[768,1024]{1,0:T(8,128)}, u32[]{:S(2)}) copy-start(s32[768,1024]{1,0:T(8,128)} %param.10) | copy-start | bytes 9437188
  165.9 227.2 %all-reduce.7.cloned.1.call-start = ((), (), s32[]{:S(2)}) async-start(), calls=%async_computation.2 | async-start | bytes 131072
  252.8 2.1 copy-start.8
  254.9 0.6 copy-start.4
Sparse Core Ops, SparseCore 0:
  166.0 19.0 reduce-scatter.2
  258.8 134.1 all-reduce.6
where the time goes:
time: 402 us; the launch traced here: 401 us
  blocking collectives  265 us (66%)
  waiting for transfers between devices  85.6 us (21%)
  other arithmetic  19.3 us (5%)
  between operations  14.2 us (4%)
  matrix products  13.5 us (3%)
    psum x1, blocking collectives, body(): lax.psum(called_proj.astype(jnp.bfloat16), 'samp').astype(jnp.float32)  124 us
    unnamed x3, waiting for transfers between devices  68.9 us
    psum x1, blocking collectives, body(): lax.psum((jnp.sum(residual * residual, axis=0), jnp.sum(direction * appli...  66.8 us
    psum x1, blocking collectives, body(): lax.psum((res_square, jnp.sum(solution_new, axis=0), jnp.sum(solution_new...  63.2 us
    reduce_scatter x1, waiting for transfers between devices, body(): lax.psum_scatter((term / VARIANTS).astype(jnp.bfloat16), 'var', scatter_d...  16.6 us
    all_gather x1, blocking collectives, body(): piece = lax.all_gather(direction_b, 'var', axis=0, tiled=True)  11.4 us
    reduce_sum x1, other arithmetic, body(): allele_sum = jnp.sum(coded, axis=1).astype(jnp.float32)  10.1 us
  transfers between devices with their start and end apart: 2, of which 2 were waited for; matrix products, arithmetic and copies ran while one was open for 1% of the time, Pallas kernels for 0%

commit v1 on v0

--- a/solution.py
+++ b/solution.py
@@ -33,7 +33,9 @@
     called_proj = jnp.dot(called_cols, piece, preferred_element_type=jnp.float32)
     raw_proj, called_proj, allele_sum, called_count = (
         lax.psum(raw_proj.astype(jnp.bfloat16), "samp").astype(jnp.float32),
-        lax.psum(called_proj.astype(jnp.bfloat16), "samp").astype(jnp.float32),
+        jnp.sum(lax.all_gather(called_proj.astype(jnp.bfloat16), "samp"), axis=0).astype(
+            jnp.float32
+        ),
         lax.psum(allele_sum.astype(jnp.bfloat16), "samp").astype(jnp.float32),
         lax.psum(called_count.astype(jnp.bfloat16), "samp").astype(jnp.float32),
     )

time: 402 us -> 493 us (1.23)
  waiting for transfers between devices: 85.6 us -> 149 us
  blocking collectives: 265 us -> 290 us
    unnamed x3, waiting for transfers between devices: 68.9 us -> 132 us
    all_gather x0 -> x1, blocking collectives: none -> 28.3 us  [body(): lax.all_gather(called_proj.astype(jnp.bfloat16), 'samp')]
where the time goes in v1:
time: 493 us
  blocking collectives  290 us (59%)
  waiting for transfers between devices  149 us (30%)
  other arithmetic  19.9 us (4%)
  matrix products  15.8 us (3%)
  between operations  14.2 us (3%)
    unnamed x3, waiting for transfers between devices  132 us
    psum x1, blocking collectives, body(): lax.psum(raw_proj.astype(jnp.bfloat16), 'samp').astype(jnp.float32)  121 us
    psum x1, blocking collectives, body(): lax.psum((jnp.sum(residual * residual, axis=0), jnp.sum(direction * appli...  66.8 us
    psum x1, blocking collectives, body(): lax.psum((res_square, jnp.sum(solution_new, axis=0), jnp.sum(solution_new...  62.7 us
    all_gather x1, blocking collectives, body(): lax.all_gather(called_proj.astype(jnp.bfloat16), 'samp')  28.3 us
    reduce_scatter x1, waiting for transfers between devices, body(): lax.psum_scatter((term / VARIANTS).astype(jnp.bfloat16), 'var', scatter_d...  17.2 us
    all_gather x1, blocking collectives, body(): piece = lax.all_gather(direction_b, 'var', axis=0, tiled=True)  11.4 us
    reduce_sum x1, other arithmetic, body(): allele_sum = jnp.sum(coded, axis=1).astype(jnp.float32)  10.1 us
  transfers between devices with their start and end apart: 2, of which 2 were waited for; matrix products, arithmetic and copies ran while one was open for 1% of the time, Pallas kernels for 0%

profile of v1, /device:TPU:1, one launch (start us, length us, event | category | flops | bytes accessed | tf_op | source)
XLA Modules:
  0.0 492.6 jit_solution(1983604037573923104)
XLA Ops:
  7.2 0.8 convert_element_type.63
  8.0 11.4 %all_gather.9 = bf16[3072,16]{0,1:T(8,128)(2,1)S(1)} all-gather(bf16[768,16]{0,1:T(8,128)(2,1)S(1)} %convert_element_type.63), channel_id=1, replica_groups=mesh['var'=4,'samp'=32] {'var'}, dimensions={0}, use_global_device_ids=true | all-gather | bytes 122880 | tf_op jit(solution)/shard_map/all_gather | solution.py:29
  19.5 5.0 %fusion.10 = bf16[768,16]{0,1:T(8,128)(2,1)S(1)} fusion(bf16[3072,16]{0,1:T(8,128)(2,1)S(1)} %all_gather.9, s32[768,3072]{1,0:T(8,128)} %param.9), kind=kOutput, calls=%fused_computation.13 | convolution fusion | flops 77869056 | bytes 9560064 | tf_op jit(solution)/shard_map/dot_general | solution.py:33
  24.5 28.3 %all-gather = bf16[24576,16]{0,1:T(8,128)(2,1)S(1)} all-gather(bf16[768,16]{0,1:T(8,128)(2,1)S(1)} %fusion.10), channel_id=2, replica_groups=mesh['var'=4,'samp'=32] {'samp'}, dimensions={0}, use_global_device_ids=true | all-gather | bytes 811008 | tf_op jit(solution)/shard_map/all_gather | solution.py:36
  53.2 10.1 %multiply_reduce_fusion = (s32[768]{0:T(1024)S(1)}, s32[768]{0:T(1024)S(1)}, bf16[768,3072]{1,0:T(8,128)(2,1)}) fusion(s32[768,3072]{1,0:T(8,128)} %param.8, s32[768,3072]{1,0:T(8,128)} %param.9), kind=kLoop, calls=%fused_computation.1 | loop fusion | flops 9435648 | bytes 23599104 | tf_op jit(solution)/shard_map/reduce_sum | solution.py:21
  63.3 3.7 convolution_convert_fusion
  67.0 120.9 %all-reduce.4 = (bf16[768,16]{0,1:T(8,128)(2,1)S(1)}, bf16[768]{0:T(1024)(128)(2,1)S(1)}, bf16[768]{0:T(1024)(128)(2,1)S(1)}) all-reduce(bf16[768,16]{0,1:T(8,128)(2,1)S(1)} %convolution_convert_fusion, bf16[768]{0:T(1024)(128)(2,1)S(1)} %get-tuple-element.41, ...), channel_id=1, replica_groups=mesh['var'=4,'samp'=32] {'samp'}, use_global_device_ids=true, to_apply=%region_2.0 | all-reduce | flops 13824 | bytes 55296 | tf_op jit(solution)/shard_map/psum | solution.py:35
  188.0 4.6 convolution_bitcast_fusion
  192.6 0.3 slice-done.1
  192.8 1.4 fusion.1
  194.4 2.3 reduce_sum.90
  196.7 17.2 %reduce-scatter.3.cloned.1.call-done = bf16[768,16]{0,1:T(8,128)(2,1)} async-done(((bf16[3072,16]{0,1:T(8,128)(2,1)}), bf16[768,16]{0,1:T(8,128)(2,1)}) %reduce-scatter.3.cloned.1.call-update) | async-done | bytes 24592 | tf_op jit(solution)/shard_map/reduce_scatter | solution.py:49
  213.9 0.9 multiply_reduce_fusion.3
  214.8 66.8 %all-reduce.3 = (f32[16]{0:T(128)S(1)}, f32[16]{0:T(128)S(1)}) all-reduce(f32[16]{0:T(128)S(1)} %multiply_reduce_fusion.4, f32[16]{0:T(128)S(1)} %multiply_reduce_fusion.3), channel_id=1, replica_groups=mesh['var'=4,'samp'=32] {'var','samp'}, use_global_device_ids=true, to_apply=%region_1.0 | all-reduce | flops 32 | bytes 256 | tf_op jit(solution)/shard_map/psum | solution.py:53
  281.6 1.6 multiply_reduce_fusion.2
  283.2 62.7 %all-reduce.2 = (f32[16]{0:T(128)S(1)}, f32[16]{0:T(128)}, f32[1024]{0:T(1024)}, f32[16]{0:T(128)S(1)}) all-reduce(f32[16]{0:T(128)S(1)} %get-tuple-element.30, f32[16]{0:T(128)S(1)} %get-tuple-element.33, f32[1024]{0:T(1024)S(1)} %convert_element_type.81, f32[16]{0:T(128)S(1)} %get-tuple-element.34), channel_id=1, replica_groups=mesh['var'=4,'samp'=32] {'var','samp'}, use_global_device_ids=true, to_apply=%region_12.0 | all-reduce | flops 1072 | bytes 8576 | tf_op jit(solution)/shard_map/psum | solution.py:61
  346.1 1.9 gather_fusion
  348.0 1.1 fusion.7
  349.1 0.7 sqrt_multiply_fusion
  349.8 1.5 multiply_add_fusion
  351.3 0.8 broadcast_multiply_fusion.1
  352.1 132.2 %all-reduce.7.cloned.1.call-done = f32[1024,16]{0,1:T(8,128)} async-done(((f32[1024,16]{0,1:T(8,128)}), f32[1024,16]{0,1:T(8,128)}) %all-reduce.7.cloned.1.call-update) | async-done | bytes 65552
  484.3 0.8 fusion.20
  485.1 0.7 copy.17
  (35 shorter events, 0.9 us)
Async XLA Ops:
  7.2 206.7 %reduce-scatter.3.cloned.1.call-start = ((), (), s32[]{:S(2)}) async-start(), calls=%async_computation.1 | async-start | bytes 122880 | tf_op jit(solution)/shard_map/reduce_scatter | solution.py:49
  63.3 129.3 %slice-start = ((s8[4718592]{0:T(1024)(128)(4,1)}), s8[524288]{0:T(1024)(128)(4,1)S(1)}, s32[]{:S(2)}) async-start(s8[4718592]{0:T(1024)(128)(4,1)} %bitcast.17), calls=%async_computation.3 | async-start | bytes 1048576
  187.9 4.9 slice-start.1
  192.5 1.8 copy-start.2
  192.5 1.9 copy-start.5
  192.5 21.4 %copy-start.1 = (f32[768,16]{0,1:T(8,128)S(1)}, f32[768,16]{0,1:T(8,128)}, u32[]{:S(2)}) copy-start(f32[768,16]{0,1:T(8,128)} %param.15) | copy-start | bytes 147460
  192.5 21.4 %copy-start.6 = (f32[16]{0:T(128)S(1)}, f32[16]{0:T(128)}, u32[]{:S(2)}) copy-start(f32[16]{0:T(128)} %param.12) | copy-start | bytes 196
  192.5 89.1 %copy-start.4 = (f32[768,16]{0,1:T(8,128)S(1)}, f32[768,16]{0,1:T(8,128)}, u32[]{:S(2)}) copy-start(f32[768,16]{0,1:T(8,128)} %param.13) | copy-start | bytes 147460
  194.2 153.8 %copy-start = (s32[768,1024]{1,0:T(8,128)S(1)}, s32[768,1024]{1,0:T(8,128)}, u32[]{:S(2)}) copy-start(s32[768,1024]{1,0:T(8,128)} %param.10) | copy-start | bytes 9437188
  194.2 290.1 %all-reduce.7.cloned.1.call-start = ((), (), s32[]{:S(2)}) async-start(), calls=%async_computation.2 | async-start | bytes 131072
  283.2 62.7 %copy-start.3 = (f32[768,16]{0,1:T(8,128)}, f32[768,16]{0,1:T(8,128)S(1)}, u32[]{:S(2)}) copy-start(f32[768,16]{0,1:T(8,128)S(1)} %get-tuple-element.35) | copy-start | bytes 147460
Sparse Core Ops, SparseCore 0:
  194.3 19.5 reduce-scatter.2
  349.2 135.0 all-reduce.6
